TPU v7x, 128 devices: a whole 4x4x4 slice. The times are simulated.
128 devices in a mesh: dp: 8 (over z, core), seq: 16 (over x, y).
Axes of the slice: x: 4, y: 4, z: 4, core: 2. Of those that a mesh axis runs over, the one named last changes fastest.
Arguments:
- tokens: bfloat16 [8, 2048, 1024], P('dp', 'seq'), may hold values from -6 to 6
- w_qkv: bfloat16 [1024, 2048], P(('dp', 'seq')), may hold values from -0.1875 to 0.1875
- w_out: bfloat16 [1024, 1024], P(('dp', 'seq')), may hold values from -1 to 1
- w_gu: bfloat16 [1024, 9216], P(('dp', 'seq')), may hold values from -0.1875 to 0.1875
- w_down: bfloat16 [1024, 4608], P(('dp', 'seq')), may hold values from -0.125 to 0.125
- gains: bfloat16 [2176], P(('dp', 'seq')), may hold values from 0.5 to 1.5
- span_order: int32 [8, 32], P('dp'), may hold values from 0 to 31, as said below
- d_out: bfloat16 [8, 2048, 1024], P('dp', 'seq'), may hold values from -6 to 6
Outputs:
- result: bfloat16 [8, 2048, 1024], P('dp', 'seq')
- d_tokens: float32 [8, 2048, 1024], P('dp', 'seq')
- g_qkv: float32 [1024, 2048], P(('dp', 'seq'))
- g_out: float32 [1024, 1024], P(('dp', 'seq'))
- g_gu: float32 [1024, 9216], P(('dp', 'seq'))
- g_down: float32 [1024, 4608], P(('dp', 'seq'))
- g_gains: float32 [2176], P(('dp', 'seq'))
Inputs may be any that keep to these rules, and one draw needn't show every extreme that they name: `span_order`: each row is a permutation of the 32 spans; slots 2 i and 2 i + 1 hold spans c and 31 - c for some c.
All inputs are finite; a program needn't handle non-finite values.
Results may differ from a plain program's by a relative error of at most 0.02.
Values may be sent and summed in bfloat16 or wider, within the bound.
No kernel may reach another device: no remote copies, remote signals or barrier semaphores. Data moves between devices by JAX's collectives and lax.ppermute only.
A program may use at most 192 MiB of HBM per device.

v0:
```python
import jax
import jax.numpy as jnp
from jax import lax
from jax.sharding import Mesh
from jax.sharding import PartitionSpec as P

H = 16
KVH = 8
HD = 64
FF = 4608
SEQ = ("seq_0", "seq_1")
DP_SEQ = ("dp", "seq_0", "seq_1")


EPSILON = 1e-05
THETA = 1000000.0


def in_one_piece(arrays, axis, dim, along):
    both = jnp.concatenate(arrays, axis=along)
    result, at, done = (lax.all_gather(both, axis, axis=dim, tiled=True), 0, [])
    for a in arrays:
        done.append(lax.slice_in_dim(result, at, at + a.shape[along], axis=along))
        at += a.shape[along]
    return tuple(done)


def sent_together(arrays, axis, split_dim, concat_dim, along):
    ends, at = ([], 0)
    for a in arrays[:-1]:
        at += a.shape[along]
        ends.append(at)
    both = jnp.concatenate(arrays, axis=along)
    return tuple(
        jnp.split(
            lax.all_to_all(both, axis, split_axis=split_dim, concat_axis=concat_dim, tiled=True),
            ends,
            axis=along,
        )
    )


def scatter_axes(shard, axes, dim):
    for axis in axes:
        shard = lax.psum_scatter(shard, axis, scatter_dimension=dim, tiled=True)
    return shard


def in_blocks(shard, dim, length):
    dims = shard.shape
    parts = shard.reshape(*dims[:dim], length, dims[dim] // length, *dims[dim + 1 :])
    return jnp.moveaxis(parts, dim, 0)


def sum_packed(arrays, axis, dims):
    length = lax.axis_size(axis)
    parts = [in_blocks(a, dim, length) for a, dim in zip(arrays, dims)]
    lines = jnp.concatenate([b.reshape(length, -1) for b in parts], axis=1)
    extent = max(16, -(-lines.shape[1] // 1024) * 8)
    lines = jnp.pad(lines, ((0, 0), (0, extent * 128 - lines.shape[1]))).reshape(-1, 128)
    vector, at, done = (lax.psum_scatter(lines, axis, tiled=True).reshape(-1), 0, [])
    for b in parts:
        part = b[0]
        done.append(vector[at : at + part.size].reshape(part.shape))
        at += part.size
    return tuple(done)


def angles(positions, width):
    half = width // 2
    freqs = THETA ** (-(jnp.arange(half, dtype=jnp.float32) * 2.0 / width))
    turned = positions.astype(jnp.float32)[:, None] * freqs[None, :]
    return (jnp.cos(turned)[:, None, :], jnp.sin(turned)[:, None, :])


def rotate(values, cosine, sine):
    half = values.shape[-1] // 2
    first = values[..., :half]
    second = values[..., half:]
    return jnp.concatenate(
        [first * cosine - second * sine, second * cosine + first * sine], axis=-1
    )


def unrotate(grads, cosine, sine):
    half = grads.shape[-1] // 2
    first = grads[..., :half]
    second = grads[..., half:]
    return jnp.concatenate(
        [first * cosine + second * sine, second * cosine - first * sine], axis=-1
    )


def rms_back(d_gained, unit, inv_scale, gain):
    d_unit = d_gained * gain
    return inv_scale * (d_unit - unit * jnp.mean(d_unit * unit, axis=-1, keepdims=True))


def masked_scores(queries, keys, q_pos, k_pos):
    scale = queries.shape[-1] ** (-0.5)
    scores = jnp.einsum("qkgd,tkd->kgqt", queries, keys, preferred_element_type=jnp.float32) * scale
    allowed = q_pos[:, None] >= k_pos[None, :]
    return jnp.where(allowed, scores, -1e30)


def on_device(tokens, w_qkv, w_out, w_gu, w_down, gains, span_order, d_out):
    seqs_here, local_len, width = tokens.shape
    rows = seqs_here * local_len
    head_dim = HD
    heads = H
    kv_heads = KVH
    group = heads // kv_heads
    kv_width = kv_heads * head_dim
    hidden_units = FF
    half_span = local_len // 2
    length = span_order.shape[1] * half_span
    scale = head_dim ** (-0.5)
    shard_rows = w_gu.shape[0]
    seq_index = lax.axis_index(SEQ)
    own_spans = lax.dynamic_slice_in_dim(span_order, 2 * seq_index, 2, 1)
    offsets = jnp.arange(local_len, dtype=jnp.int32)
    own_pos = own_spans[:, offsets // half_span] * half_span + offsets % half_span
    spots = jnp.arange(length, dtype=jnp.int32)
    every_pos = span_order[:, spots // half_span] * half_span + spots % half_span
    cosine, sine = angles(own_pos.reshape(rows), head_dim)
    qkv_full, out_full, gain_full = (
        *in_one_piece((w_qkv, w_out), DP_SEQ, 0, 1),
        lax.all_gather(gains, DP_SEQ, axis=0, tiled=True),
    )
    gain_all = gain_full.astype(jnp.float32)
    a_gain = gain_all[:width]
    f_gain = gain_all[width : 2 * width]
    q_gain = gain_all[2 * width : 2 * width + head_dim]
    k_gain = gain_all[2 * width + head_dim :]
    inputs = tokens.reshape(rows, width).astype(jnp.float32)
    scale_one = lax.rsqrt(jnp.mean(inputs * inputs, axis=-1, keepdims=True) + EPSILON)
    unit_one = inputs * scale_one
    normed_one = (unit_one * a_gain).astype(jnp.bfloat16)
    mixed = jnp.dot(normed_one, qkv_full, preferred_element_type=jnp.float32)
    q_raw = mixed[:, :width].reshape(rows, heads, head_dim)
    k_raw = mixed[:, width : width + kv_width].reshape(rows, kv_heads, head_dim)
    v_raw = mixed[:, width + kv_width :]
    q_scale = lax.rsqrt(jnp.mean(q_raw * q_raw, axis=-1, keepdims=True) + EPSILON)
    q_unit = q_raw * q_scale
    q_rot = rotate(q_unit * q_gain, cosine, sine).astype(jnp.bfloat16)
    k_scale = lax.rsqrt(jnp.mean(k_raw * k_raw, axis=-1, keepdims=True) + EPSILON)
    k_unit = k_raw * k_scale
    k_rot = rotate(k_unit * k_gain, cosine, sine).astype(jnp.bfloat16)
    kv_local = jnp.concatenate([k_rot.reshape(rows, kv_width), v_raw.astype(jnp.bfloat16)], axis=1)
    kv_every = lax.all_gather(
        kv_local.reshape(seqs_here, local_len, 2 * kv_width), SEQ, axis=1, tiled=True
    )
    q_groups = q_rot.reshape(seqs_here, local_len, kv_heads, group, head_dim)

    def forward_one(items):
        queries, keyvals, q_pos, k_pos = items
        keys = keyvals[:, :kv_width].reshape(length, kv_heads, head_dim)
        values = keyvals[:, kv_width:].reshape(length, kv_heads, head_dim)
        scores = masked_scores(queries, keys, q_pos, k_pos)
        top = jnp.max(scores, axis=-1, keepdims=True)
        weights = jnp.exp(scores - top)
        total = jnp.sum(weights, axis=-1, keepdims=True)
        probs = weights / total
        attended = jnp.einsum(
            "kgqt,tkd->qkgd", probs.astype(jnp.bfloat16), values, preferred_element_type=jnp.float32
        )
        return (attended, top + jnp.log(total))

    attended, log_total = lax.map(forward_one, (q_groups, kv_every, own_pos, every_pos))
    attn_out = attended.reshape(rows, width).astype(jnp.bfloat16)
    middle = inputs + jnp.dot(attn_out, out_full, preferred_element_type=jnp.float32)
    scale_two = lax.rsqrt(jnp.mean(middle * middle, axis=-1, keepdims=True) + EPSILON)
    unit_two = middle * scale_two
    normed_two = (unit_two * f_gain).astype(jnp.bfloat16)
    gu_piece, down_piece = sent_together(
        (w_gu.reshape(shard_rows, 2, hidden_units), w_down.reshape(shard_rows, 1, hidden_units)),
        SEQ,
        2,
        0,
        1,
    )
    gu_cols, down_cols = in_one_piece((gu_piece, down_piece), "dp", 0, 1)
    down_cols = down_cols[:, 0, :]
    normed_all, d_all = in_one_piece(
        (normed_two.reshape(seqs_here, local_len, width), d_out), SEQ, 1, 0
    )
    every_rows = normed_all.shape[0] * normed_all.shape[1]
    normed_all = normed_all.reshape(every_rows, width)
    d_all = d_all.reshape(every_rows, width)
    gate_up = jnp.einsum("rd,dgc->rgc", normed_all, gu_cols, preferred_element_type=jnp.float32)
    gate = gate_up[:, 0, :]
    upper = gate_up[:, 1, :]
    sigma = jax.nn.sigmoid(gate)
    swish = gate * sigma
    activated = (swish * upper).astype(jnp.bfloat16)
    partial_out = jnp.einsum("rc,dc->rd", activated, down_cols, preferred_element_type=jnp.float32)
    down_sum = scatter_axes(
        partial_out.reshape(seqs_here, every_rows // seqs_here, width).astype(jnp.bfloat16), SEQ, 1
    ).astype(jnp.float32)
    result = middle + down_sum.reshape(rows, width)
    d_act = (
        jnp.dot(d_all, down_cols, preferred_element_type=jnp.float32)
        .astype(jnp.bfloat16)
        .astype(jnp.float32)
    )
    g_down_cols = jnp.einsum("rd,rc->dc", d_all, activated, preferred_element_type=jnp.float32)
    d_gate = d_act * upper * (sigma * (1.0 + gate * (1.0 - sigma)))
    d_upper = d_act * swish
    d_gate_up = jnp.stack([d_gate, d_upper], axis=1).astype(jnp.bfloat16)
    g_gu_cols = jnp.einsum("rd,rgc->dgc", normed_all, d_gate_up, preferred_element_type=jnp.float32)
    d_normed_part = jnp.einsum(
        "rgc,dgc->rd", d_gate_up, gu_cols, preferred_element_type=jnp.float32
    )
    d_normed_two = (
        lax.psum_scatter(
            d_normed_part.reshape(seqs_here, every_rows // seqs_here, width).astype(jnp.bfloat16),
            SEQ,
            scatter_dimension=1,
            tiled=True,
        )
        .astype(jnp.float32)
        .reshape(rows, width)
    )
    g_gu_rows, g_down_rows = tuple(
        (
            part.astype(jnp.float32)
            for part in sum_packed(
                (g_gu_cols.astype(jnp.bfloat16), g_down_cols[:, None, :].astype(jnp.bfloat16)),
                "dp",
                (0, 0),
            )
        )
    )
    g_gu_back, g_down_back = tuple(
        (
            part.astype(jnp.float32)
            for part in sent_together(
                (g_gu_rows.astype(jnp.bfloat16), g_down_rows.astype(jnp.bfloat16)), SEQ, 0, 2, 1
            )
        )
    )
    g_gu_shard = g_gu_back.reshape(shard_rows, 2 * hidden_units)
    g_down_shard = g_down_back.reshape(shard_rows, hidden_units)
    g_f_gain = jnp.sum(d_normed_two * unit_two, axis=0)
    d_result_full = d_out.reshape(rows, width).astype(jnp.float32)
    d_middle = d_result_full + rms_back(d_normed_two, unit_two, scale_two, f_gain)
    qkv_back, out_back = (qkv_full, out_full)
    d_branch = d_middle.astype(jnp.bfloat16)
    g_out = jnp.einsum("rd,re->de", attn_out, d_branch, preferred_element_type=jnp.float32)
    d_attended = jnp.einsum(
        "re,de->rd", d_branch, out_back, preferred_element_type=jnp.float32
    ).astype(jnp.bfloat16)
    d_groups = d_attended.reshape(seqs_here, local_len, kv_heads, group, head_dim)

    def backward_one(items):
        queries, keyvals, q_pos, k_pos, lse, d_att = items
        keys = keyvals[:, :kv_width].reshape(length, kv_heads, head_dim)
        values = keyvals[:, kv_width:].reshape(length, kv_heads, head_dim)
        scores = masked_scores(queries, keys, q_pos, k_pos)
        probs = jnp.exp(scores - lse)
        d_probs = jnp.einsum("qkgd,tkd->kgqt", d_att, values, preferred_element_type=jnp.float32)
        delta = jnp.sum(probs * d_probs, axis=-1, keepdims=True)
        d_scores = (probs * (d_probs - delta)).astype(jnp.bfloat16)
        d_queries = (
            jnp.einsum("kgqt,tkd->qkgd", d_scores, keys, preferred_element_type=jnp.float32) * scale
        )
        d_keys = (
            jnp.einsum("kgqt,qkgd->tkd", d_scores, queries, preferred_element_type=jnp.float32)
            * scale
        )
        d_values = jnp.einsum(
            "kgqt,qkgd->tkd", probs.astype(jnp.bfloat16), d_att, preferred_element_type=jnp.float32
        )
        return (
            d_queries,
            jnp.concatenate(
                [d_keys.reshape(length, kv_width), d_values.reshape(length, kv_width)], axis=1
            ),
        )

    d_queries, d_kv_terms = lax.map(
        backward_one, (q_groups, kv_every, own_pos, every_pos, log_total, d_groups)
    )
    d_kv = (
        lax.psum_scatter(d_kv_terms.astype(jnp.bfloat16), SEQ, scatter_dimension=1, tiled=True)
        .astype(jnp.float32)
        .reshape(rows, 2 * kv_width)
    )
    d_q_gained = unrotate(d_queries.reshape(rows, heads, head_dim), cosine, sine)
    g_q_gain = jnp.sum(d_q_gained * q_unit, axis=(0, 1))
    d_q_raw = rms_back(d_q_gained, q_unit, q_scale, q_gain)
    d_k_gained = unrotate(d_kv[:, :kv_width].reshape(rows, kv_heads, head_dim), cosine, sine)
    g_k_gain = jnp.sum(d_k_gained * k_unit, axis=(0, 1))
    d_k_raw = rms_back(d_k_gained, k_unit, k_scale, k_gain)
    d_mixed = jnp.concatenate(
        [d_q_raw.reshape(rows, width), d_k_raw.reshape(rows, kv_width), d_kv[:, kv_width:]], axis=1
    ).astype(jnp.bfloat16)
    g_qkv = jnp.einsum("rd,rf->df", normed_one, d_mixed, preferred_element_type=jnp.float32)
    d_normed_one = jnp.einsum("rf,df->rd", d_mixed, qkv_back, preferred_element_type=jnp.float32)
    g_a_gain = jnp.sum(d_normed_one * unit_one, axis=0)
    d_inputs = d_middle + rms_back(d_normed_one, unit_one, scale_one, a_gain)
    g_gain_all = jnp.concatenate([g_a_gain, g_f_gain, g_q_gain, g_k_gain])
    g_qkv_shard, g_out_shard, g_gains_shard = sum_packed(
        (g_qkv, g_out, g_gain_all), DP_SEQ, (0, 0, 0)
    )
    return (
        result.astype(jnp.bfloat16).reshape(seqs_here, local_len, width),
        d_inputs.reshape(seqs_here, local_len, width),
        g_qkv_shard,
        g_out_shard,
        g_gu_shard,
        g_down_shard,
        g_gains_shard,
    )


def solution(mesh):
    split = Mesh(mesh.devices.reshape(mesh.shape["dp"], 4, 4), ("dp", "seq_0", "seq_1"))
    return jax.shard_map(
        on_device,
        mesh=split,
        in_specs=(
            P("dp", SEQ, None),
            P(DP_SEQ, None),
            P(DP_SEQ, None),
            P(DP_SEQ, None),
            P(DP_SEQ, None),
            P(DP_SEQ),
            P("dp", None),
            P("dp", SEQ, None),
        ),
        out_specs=(
            P("dp", SEQ, None),
            P("dp", SEQ, None),
            P(DP_SEQ, None),
            P(DP_SEQ, None),
            P(DP_SEQ, None),
            P(DP_SEQ, None),
            P(DP_SEQ),
        ),
        check_vma=False,
    )
```

profile of v0, /device:TPU:0, one launch (start us, length us, event | category | flops | bytes accessed | tf_op | source)
XLA Modules:
  0.0 781.4 jit_solution(1209340535536893932)
XLA Ops:
  9.6 68.9 %all-reduce.1 = bf16[2176]{0:T(1024)(128)(2,1)S(1)} all-reduce(bf16[2176]{0:T(1024)(128)(2,1)S(1)} %dynamic-update-slice), channel_id=1, replica_groups=mesh['dp'=8,'seq_0'=4,'seq_1'=4] {'dp','seq_0','seq_1'}, use_global_device_ids=true, to_apply=%add.1 | all-reduce | flops 2176 | bytes 8704
  88.1 4.9 copy.163
  93.0 7.8 reshape.762
  112.1 15.7 %fusion.77 = s32[2048]{0:T(1024)S(1)} fusion(pred[2048]{0:T(1024)(128)(4,1)S(1)} %compare_reduce_fusion, pred[2048]{0:T(1024)(128)(4,1)S(1)} %compare_reduce_fusion.1, pred[2048]{0:T(1024)(128)(4,1)S(1)} %compare_reduce_fusion.2, pred[2048]{0:T(1024)(128)(4,1)S(1)} %compare_reduce_fusion.3, pred[2048]{0:T(1024)(128)(4,1)S(1)} %compare_reduce_fusion.4, ...), kind=kLoop, calls=%fused_computation.174 | loop fusion | flops 67584 | bytes 67684 | tf_op jit(solution)/shard_map/add | solution.py:124
  128.1 6.1 reshape.763
  134.3 5.7 copy.198
  153.5 7.3 fusion.98
  160.8 8.3 %fusion.3 = f32[8,2,128]{2,1,0:T(2,128)S(1)} fusion(f32[8,2,128,2048]{2,3,1,0:T(8,128)} %get-tuple-element.126, f32[8,2,128]{2,1,0:T(2,128)S(1)} %get-tuple-element.125), kind=kLoop, calls=%fused_computation.9 | loop fusion | flops 8386560 | bytes 16793600 | tf_op jit(solution)/shard_map/while/body/eval_jaxpr/reduce_sum | solution.py:162
  169.2 7.4 fusion.42
  180.9 70.4 %all-gather.8.cloned.1.call-done = bf16[2,2048,1024]{2,1,0:T(8,128)(2,1)} async-done(((bf16[2,128,1024]{2,1,0:T(8,128)(2,1)}), bf16[2,2048,1024]{2,1,0:T(8,128)(2,1)}) %all-gather.8.cloned.1.call-update) | async-done | bytes 8388624 | tf_op jit(solution)/shard_map/all_gather | solution.py:21
  260.0 5.5 convert_bitcast_fusion
  265.7 5.9 fusion.46
  273.1 5.0 fusion.18
  278.1 34.0 %reduce-scatter.6.cloned.1.call-done = bf16[1,512,1024]{2,1,0:T(8,128)(2,1)} async-done(((bf16[1,2048,1024]{2,1,0:T(8,128)(2,1)}), bf16[1,512,1024]{2,1,0:T(8,128)(2,1)}) %reduce-scatter.6.cloned.1.call-update) | async-done | bytes 1048592 | tf_op jit(solution)/shard_map/reduce_scatter | solution.py:45
  325.4 6.5 fusion.34
  331.9 5.0 copy.184
  336.9 5.5 reshape.760
  355.2 37.7 %reduce-scatter.10.cloned.1.call-done = bf16[1,128,1024]{2,1,0:T(8,128)(2,1)} async-done(((bf16[1,2048,1024]{2,1,0:T(8,128)(2,1)}), bf16[1,128,1024]{2,1,0:T(8,128)(2,1)}) %reduce-scatter.10.cloned.1.call-update) | async-done | bytes 262160 | tf_op jit(solution)/shard_map/reduce_scatter | solution.py:215
  395.3 23.0 %reduce-scatter.8.cloned.1.call-done = bf16[1,128,1024]{2,1,0:T(8,128)(2,1)} async-done(((bf16[1,512,1024]{2,1,0:T(8,128)(2,1)}), bf16[1,128,1024]{2,1,0:T(8,128)(2,1)}) %reduce-scatter.8.cloned.1.call-update) | async-done | bytes 262160 | tf_op jit(solution)/shard_map/reduce_scatter | solution.py:45
  423.8 13.8 %fusion = (f32[8,2,128]{2,1,0:T(2,128)S(1)}, f32[8,2048,128,2]{2,1,3,0:T(8,128)}) fusion(f32[8,2,128,2048]{2,3,1,0:T(8,128)} %get-tuple-element.126, f32[8,2,128]{2,1,0:T(2,128)} %bitcast.266, bf16[2048,8,64,1]{0,2,3,1:T(8,128)(2,1)} %bitcast.242, bf16[128,8,2,64]{0,3,2,1:T(8,128)(2,1)S(1)} %bitcast.246), kind=kOutput, calls=%fused_computation.2 | convolution fusion | flops 549451776 | bytes 35930112 | tf_op jit(solution)/shard_map/while/body/eval_jaxpr/qkgd,tkd->kgqt/dot_general | solution.py:261
  437.6 9.8 %bitcast_convert_fusion.1 = bf16[8,64,2048]{2,1,0:T(8,128)(2,1)} fusion(bf16[128,8,2,64]{0,3,2,1:T(8,128)(2,1)S(1)} %bitcast.247, f32[8,2,128,2048]{2,3,1,0:T(8,128)} %get-tuple-element.126, f32[8,2,128]{2,1,0:T(2,128)S(1)} %bitcast.267), kind=kOutput, calls=%fused_computation.21 | convolution fusion | flops 546308096 | bytes 19144704 | tf_op jit(solution)/shard_map/while/body/eval_jaxpr/kgqt,qkgd->tkd/dot_general | solution.py:271
  447.4 12.0 %fusion.2 = bf16[8,2,128,2048]{2,3,1,0:T(8,128)(2,1)S(1)} fusion(f32[8,2048,128,2]{2,1,3,0:T(8,128)} %get-tuple-element.130, f32[8,2,128,2048]{2,3,1,0:T(8,128)} %get-tuple-element.126, f32[8,2,128]{2,1,0:T(2,128)S(1)} %get-tuple-element.129, f32[8,2,128]{2,1,0:T(2,128)S(1)} %bitcast.268), kind=kLoop, calls=%fused_computation.4 | loop fusion | flops 16777216 | bytes 41959424 | tf_op jit(solution)/shard_map/while/body/eval_jaxpr/convert_element_type | solution.py:263
  482.5 5.1 convolution_multiply_fusion
  493.4 5.1 reshape_reshape.13
  499.1 54.4 %reduce-scatter.12.cloned.1.call-done = bf16[1,128,1024]{2,1,0:T(8,128)(2,1)} async-done(((bf16[1,2048,1024]{2,1,0:T(8,128)(2,1)}), bf16[1,128,1024]{2,1,0:T(8,128)(2,1)}) %reduce-scatter.12.cloned.1.call-update) | async-done | bytes 262160 | tf_op jit(solution)/shard_map/reduce_scatter | solution.py:285
  556.5 5.2 fusion.70
  561.8 9.4 %reshape_reshape.12 = f32[128,16384]{1,0:T(8,128)} reshape(f32[1024,2048]{1,0:T(8,128)} %fusion.70) | data formatting | bytes 16777216 | tf_op jit(solution)/shard_map/reshape;reshape | solution.py:58
  575.4 9.6 %select_maximum_fusion = f32[128,25600]{1,0:T(8,128)} fusion(f32[128,17]{1,0:T(8,128)S(1)} %reshape.483, f32[128,8192]{1,0:T(8,128)} %reshape_reshape.13, f32[128,16384]{1,0:T(8,128)} %reshape_reshape.12), kind=kLoop, calls=%fused_computation.10 | loop fusion | flops 19660800 | bytes 25698816 | tf_op jit(solution)/shard_map/concatenate | solution.py:58
  585.0 12.1 %reshape.484 = f32[25600,128]{1,0:T(8,128)} reshape(f32[128,25600]{1,0:T(8,128)} %select_maximum_fusion) | data formatting | bytes 26214400 | tf_op jit(solution)/shard_map/reshape | solution.py:60
  600.7 5.0 all-to-all-start.1
  605.7 10.8 %all-to-all-done.1 = bf16[128,3,288]{2,1,0:T(4,128)(2,1)S(1)} async-done(((bf16[128,3,288]{2,1,0:T(4,128)(2,1)}), bf16[128,3,288]{2,1,0:T(4,128)(2,1)S(1)}, u32[]{:S(2)}, u32[]{:S(2)}) %all-to-all-start.1) | async-done | bytes 221216 | tf_op jit(solution)/shard_map/all_to_all | solution.py:36
  619.3 150.4 %all-reduce.5.cloned.1.call-done = f32[25600,128]{1,0:T(8,128)} async-done(((f32[25600,128]{1,0:T(8,128)}), f32[25600,128]{1,0:T(8,128)}) %all-reduce.5.cloned.1.call-update) | async-done | bytes 13107216
  (252 shorter events, 132.3 us)
Async XLA Ops:
  7.2 75.9 %all-gather.6.cloned.1.call-start = ((), (), s32[]{:S(2)}) async-start(), calls=%async_computation.7 | async-start | bytes 6340608 | tf_op jit(solution)/shard_map/all_gather | solution.py:21
  8.6 133.4 %all-gather.12.cloned.1.call-start = ((), (), s32[]{:S(2)}) async-start(), calls=%async_computation.15 | async-start | bytes 4456448 | tf_op jit(solution)/shard_map/all_gather | solution.py:150
  82.2 59.5 %copy-start.34 = (f32[64]{0:T(128)}, f32[64]{0:T(128)S(1)}, u32[]{:S(2)}) copy-start(f32[64]{0:T(128)S(1)} %get-tuple-element.87) | copy-start | bytes 772
  83.0 58.9 %copy-start.18 = (f32[128,32]{0,1:T(8,128)}, f32[128,32]{0,1:T(8,128)S(1)}, u32[]{:S(2)}) copy-start(f32[128,32]{0,1:T(8,128)S(1)} %get-tuple-element.90) | copy-start | bytes 49156
  86.2 55.2 %copy-start.8 = (f32[128,2048]{1,0:T(8,128)}, f32[128,2048]{1,0:T(8,128)S(1)}, u32[]{:S(2)}) copy-start(f32[128,2048]{1,0:T(8,128)S(1)} %fusion.16) | copy-start | bytes 3145732
  86.4 6.6 copy-start.6
  88.1 18.2 %copy-start.17 = (s32[1,32]{1,0:T(1,128)S(1)}, s32[1,32]{1,0:T(1,128)}, u32[]{:S(2)}) copy-start(s32[1,32]{1,0:T(1,128)} %param.14) | copy-start | bytes 388
  100.8 27.4 %all-to-all-start = ((bf16[16,2,3456]{2,1,0:T(2,128)(2,1)}), bf16[16,2,3456]{2,1,0:T(2,128)(2,1)S(1)}, u32[]{:S(2)}, u32[]{:S(2)}) async-start(bf16[16,2,3456]{2,1,0:T(2,128)(2,1)} %reshape.762), calls=%async_computation | async-start | bytes 442368 | tf_op jit(solution)/shard_map/all_to_all | solution.py:36
  105.0 75.9 %all-gather.10.cloned.1.call-start = ((), (), s32[]{:S(2)}) async-start(), calls=%async_computation.9 | async-start | bytes 1990656 | tf_op jit(solution)/shard_map/all_gather | solution.py:21
  140.9 110.5 %all-gather.8.cloned.1.call-start = ((), (), s32[]{:S(2)}) async-start(), calls=%async_computation.8 | async-start | bytes 8912896 | tf_op jit(solution)/shard_map/all_gather | solution.py:21
  142.0 11.5 %copy-start.10 = (bf16[128,16,32]{0,2,1:T(8,128)(2,1)}, bf16[128,16,32]{0,2,1:T(8,128)(2,1)S(1)}, u32[]{:S(2)}) copy-start(bf16[128,16,32]{0,2,1:T(8,128)(2,1)S(1)} %get-tuple-element.72) | copy-start | bytes 393220
  160.8 8.3 %copy-start.27 = (f32[8,2,128]{2,1,0:T(2,128)}, f32[8,2,128]{2,1,0:T(2,128)S(1)}, u32[]{:S(2)}) copy-start(f32[8,2,128]{2,1,0:T(2,128)S(1)} %get-tuple-element.125) | copy-start | bytes 24580
  160.8 8.3 %copy-start.1 = (bf16[2048,512]{0,1:T(8,128)(2,1)S(1)}, bf16[2048,512]{0,1:T(8,128)(2,1)}, u32[]{:S(2)}) copy-start(bf16[2048,512]{0,1:T(8,128)(2,1)} %copy.158) | copy-start | bytes 6291460
  169.1 7.5 copy-start.31
  169.1 8.1 %copy-start.2 = (bf16[1,128,1024]{2,1,0:T(8,128)(2,1)S(1)}, bf16[1,128,1024]{2,1,0:T(8,128)(2,1)}, u32[]{:S(2)}) copy-start(bf16[1,128,1024]{2,1,0:T(8,128)(2,1)} %param.8) | copy-start | bytes 786436
  169.2 10.3 %copy-start.30 = (f32[1024]{0:T(1024)S(1)}, f32[1024]{0:T(1024)}, u32[]{:S(2)}) copy-start(f32[1024]{0:T(1024)} %get-tuple-element.85) | copy-start | bytes 12292
  169.2 10.8 %copy-start.16 = (bf16[1,128,1024]{2,1,0:T(8,128)(2,1)S(1)}, bf16[1,128,1024]{2,1,0:T(8,128)(2,1)}, u32[]{:S(2)}) copy-start(bf16[1,128,1024]{2,1,0:T(8,128)(2,1)} %param.15) | copy-start | bytes 786436
  180.8 131.3 %reduce-scatter.6.cloned.1.call-start = ((), (), s32[]{:S(2)}) async-start(), calls=%async_computation.10 | async-start | bytes 5242880 | tf_op jit(solution)/shard_map/reduce_scatter | solution.py:45
  265.5 127.5 %reduce-scatter.10.cloned.1.call-start = ((), (), s32[]{:S(2)}) async-start(), calls=%async_computation.12 | async-start | bytes 4456448 | tf_op jit(solution)/shard_map/reduce_scatter | solution.py:215
  265.7 7.4 copy-start.41
  278.1 140.2 %reduce-scatter.8.cloned.1.call-start = ((), (), s32[]{:S(2)}) async-start(), calls=%async_computation.11 | async-start | bytes 1310720 | tf_op jit(solution)/shard_map/reduce_scatter | solution.py:45
  312.1 241.3 %reduce-scatter.12.cloned.1.call-start = ((), (), s32[]{:S(2)}) async-start(), calls=%async_computation.13 | async-start | bytes 4456448 | tf_op jit(solution)/shard_map/reduce_scatter | solution.py:285
  423.8 13.8 %copy-start.26 = (f32[2,8,128]{2,1,0:T(8,128)S(1)}, f32[2,8,128]{2,1,0:T(8,128)}, u32[]{:S(2)}) copy-start(f32[2,8,128]{2,1,0:T(8,128)} %log_add_fusion) | copy-start | bytes 24580
  447.4 12.0 %copy-start.11 = (bf16[128,16,32]{0,2,1:T(8,128)(2,1)S(1)}, bf16[128,16,32]{0,2,1:T(8,128)(2,1)}, u32[]{:S(2)}) copy-start(bf16[128,16,32]{0,2,1:T(8,128)(2,1)} %copy-done.10) | copy-start | bytes 393220
  476.1 121.1 %reduce-scatter.14.cloned.1.call-start = ((), (), s32[]{:S(2)}) async-start(), calls=%async_computation.14 | async-start | bytes 1990656 | tf_op jit(solution)/shard_map/reduce_scatter | solution.py:61
  482.5 287.3 %all-reduce.5.cloned.1.call-start = ((), (), s32[]{:S(2)}) async-start(), calls=%async_computation.16 | async-start | bytes 26214400
  493.4 61.1 %copy-start.20 = (f32[128,32]{0,1:T(8,128)S(1)}, f32[128,32]{0,1:T(8,128)}, u32[]{:S(2)}) copy-start(f32[128,32]{0,1:T(8,128)} %copy-done.18) | copy-start | bytes 49156
  493.4 61.2 %copy-start.7 = (f32[128,512]{0,1:T(8,128)S(1)}, f32[128,512]{0,1:T(8,128)}, u32[]{:S(2)}) copy-start(f32[128,512]{0,1:T(8,128)} %copy-done.6) | copy-start | bytes 786436
  493.4 62.3 %copy-start.13 = (f32[128,512]{1,0:T(8,128)S(1)}, f32[128,512]{1,0:T(8,128)}, u32[]{:S(2)}) copy-start(f32[128,512]{1,0:T(8,128)} %copy.181) | copy-start | bytes 786436
  561.8 9.5 %copy-start.22 = (f32[1024]{0:T(1024)S(1)}, f32[1024]{0:T(1024)}, u32[]{:S(2)}) copy-start(f32[1024]{0:T(1024)} %copy-done.21) | copy-start | bytes 12292
  561.8 9.5 %copy-start.38 = (f32[128]{0:T(128)S(1)}, f32[128]{0:T(128)}, u32[]{:S(2)}) copy-start(f32[128]{0:T(128)} %copy-done.37) | copy-start | bytes 1540
  600.7 15.8 %all-to-all-start.1 = ((bf16[128,3,288]{2,1,0:T(4,128)(2,1)}), bf16[128,3,288]{2,1,0:T(4,128)(2,1)S(1)}, u32[]{:S(2)}, u32[]{:S(2)}) async-start(bf16[128,3,288]{2,1,0:T(4,128)(2,1)} %pad_maximum_fusion.8), calls=%async_computation.6 | async-start | bytes 786432 | tf_op jit(solution)/shard_map/all_to_all | solution.py:36
  (24 other events, 73.6 us)
Sparse Core Ops, SparseCore 0:
  11.6 71.2 all-gather.5
  87.6 48.8 all-gather.11
  141.0 26.0 all-gather.9
  181.0 70.3 all-gather.7
  265.6 46.4 reduce-scatter.5
  315.7 77.2 reduce-scatter.9
  395.3 22.9 reduce-scatter.7
  476.2 77.1 reduce-scatter.11
  555.8 32.6 reduce-scatter.13
  597.3 172.4 all-reduce.4
where the time goes:
time: 790 us; the launch traced here: 781 us
  waiting for transfers between devices  381 us (48%)
  local copies, waits for them, and re-layouts  126 us (16%)
  matrix products  99.3 us (13%)
  other arithmetic  80.4 us (10%)
  blocking collectives  68.9 us (9%)
  between operations  15.6 us (2%)
  starting transfers between devices  10.3 us (1%)
    unnamed x11, waiting for transfers between devices  151 us
    all_gather x3, waiting for transfers between devices, in_one_piece(): result, at, done = (lax.all_gather(both, axis, axis=dim, tiled=True), 0, [])  70.5 us
    unnamed x1, blocking collectives  68.9 us
    reduce_scatter x2, waiting for transfers between devices, scatter_axes(): shard = lax.psum_scatter(shard, axis, scatter_dimension=dim, tiled=True)  57 us
    reduce_scatter x1, waiting for transfers between devices, on_device(): lax.psum_scatter(d_kv_terms.astype(jnp.bfloat16), SEQ, scatter_dimension=...  54.4 us
    reduce_scatter x1, waiting for transfers between devices, on_device(): lax.psum_scatter(d_normed_part.reshape(seqs_here, every_rows // seqs_here...  37.7 us
    unnamed x93, local copies, waits for them, and re-layouts  26.9 us
    another operation x4, local copies, waits for them, and re-layouts, sum_packed(): lines = jnp.concatenate([b.reshape(length, -1) for b in parts], axis=1)  20.3 us
  transfers between devices with their start and end apart: 12, of which 7 were waited for; matrix products, arithmetic and copies ran while one was open for 28% of the time, Pallas kernels for 0%

commit v1 on v0

v1 whole, which is shorter than its diff:
```python
import jax
import jax.numpy as jnp
import numpy as np
from jax import lax
from jax.sharding import Mesh
from jax.sharding import PartitionSpec as P

D = 1024
H = 16
KVH = 8
HD = 64
FF = 4608
LOC = 128
SPAN = 64
SPANS = 32
DP = ("z", "core")
SEQ = ("x", "y")
ALL = ("z", "core", "x", "y")
UNITS = FF // 8
PAD = 640

EPSILON = 1e-05
THETA = 1000000.0
BF = jnp.bfloat16
F32 = jnp.float32

UP = [(i, (i + 1) % 4) for i in range(4)]
DOWN = [(i, (i - 1) % 4) for i in range(4)]
SWAP = [(0, 1), (1, 0)]


def gather_dp(x):
    half = x.shape[0] // 2
    a = lax.ppermute(x, "z", UP)
    b = lax.ppermute(x, "z", DOWN)
    c0 = lax.ppermute(a[:half], "z", UP)
    c1 = lax.ppermute(b[half:], "z", DOWN)
    x_, a_, b_, c0_, c1_ = [lax.ppermute(v, "core", SWAP) for v in (x, a, b, c0, c1)]
    return [x, x_, a, a_, jnp.concatenate([c0, c1]), jnp.concatenate([c0_, c1_]), b, b_]


def scatter_dp(keep, give):
    half = keep.shape[1] // 2
    got = lax.ppermute(give, "core", SWAP)
    s = (keep.astype(F32) + got.astype(F32)).astype(BF)
    r0 = lax.ppermute(s[2, :half], "z", UP)
    r1 = lax.ppermute(s[2, half:], "z", DOWN)
    e3 = lax.ppermute(s[3, half:], "z", UP)
    e1 = lax.ppermute(s[1, :half], "z", DOWN)
    f3 = lax.ppermute((s[3, :half].astype(F32) + r0.astype(F32)).astype(BF), "z", UP)
    f1 = lax.ppermute((s[1, half:].astype(F32) + r1.astype(F32)).astype(BF), "z", DOWN)
    top = s[0, :half].astype(F32) + f3.astype(F32) + e1.astype(F32)
    low = s[0, half:].astype(F32) + e3.astype(F32) + f1.astype(F32)
    return jnp.concatenate([top, low])


def swap_all(x, axes):
    return lax.all_to_all(x, axes, split_axis=0, concat_axis=0, tiled=True)


def angles(positions):
    half = HD // 2
    freqs = THETA ** (-(jnp.arange(half, dtype=F32) * 2.0 / HD))
    turned = positions.astype(F32)[..., None] * freqs
    return jnp.cos(turned), jnp.sin(turned)


def rotate(values, cosine, sine):
    half = HD // 2
    a = values[..., :half]
    b = values[..., half:]
    return jnp.concatenate([a * cosine - b * sine, b * cosine + a * sine], axis=-1)


def unrotate(values, cosine, sine):
    return rotate(values, cosine, -sine)


def inv_rms(x):
    return lax.rsqrt(jnp.mean(x * x, axis=-1, keepdims=True) + EPSILON)


def rms_back(d_gained, unit, inv_scale, gain):
    d_unit = d_gained * gain
    return inv_scale * (d_unit - unit * jnp.mean(d_unit * unit, axis=-1, keepdims=True))


def dot(spec, a, b):
    return jnp.einsum(spec, a, b, preferred_element_type=F32)


def to_slots(x):
    return x.reshape(16, 2, 64, 64).transpose(0, 2, 1, 3).reshape(16, 64, 128)


def from_slots(x):
    return x.reshape(16, 64, 2, 64).transpose(0, 2, 1, 3).reshape(2048, 64)


def on_device(tokens, w_qkv, w_out, w_gu, w_down, gains, span_order, d_out):
    z = lax.axis_index("z")
    core = lax.axis_index("core")
    s = lax.axis_index(SEQ)
    rel = np.arange(8)
    b_of = 2 * ((z - rel // 2) % 4) + (core ^ (rel % 2))
    ab = np.arange(8)
    r_of = 2 * ((z - ab // 2) % 4) + (core ^ (ab % 2))

    wq = w_qkv[:, :1024].reshape(8, 8, 128)
    wkv = jnp.concatenate(
        [w_qkv[:, 1024:1536].reshape(8, 8, 64), w_qkv[:, 1536:].reshape(8, 8, 64)], axis=-1
    )
    extra = jnp.concatenate([gains, span_order[0].astype(BF), jnp.zeros((79,), BF)])
    pay = jnp.concatenate(
        [wq.transpose(1, 0, 2), wkv.transpose(1, 0, 2), jnp.broadcast_to(extra, (8, 8, 128))], axis=1
    )
    pay = jnp.broadcast_to(pay[:, None], (8, 16, 24, 128)).reshape(128, 24, 128)
    got = swap_all(pay, ALL)
    w_j = jnp.concatenate(
        [got[:, :8].reshape(1024, 128), got[:, 8:16].reshape(1024, 128)], axis=1
    )
    gain_all = got[:, 16, :17].reshape(2176).astype(F32)
    orders = got.reshape(8, 16, 24, 128)[:, 0, 16, 17:49].astype(jnp.int32)
    a_gain = gain_all[:1024]
    f_gain = gain_all[1024:2048]
    q_gain = gain_all[2048:2112]
    k_gain = gain_all[2112:]

    x_all = jnp.concatenate(gather_dp(tokens[0])).astype(F32)

    def cut(w):
        return jnp.pad(w.reshape(8, 8, UNITS), ((0, 0), (0, 0), (0, PAD - UNITS))).transpose(1, 0, 2)

    ff_pay = jnp.concatenate([cut(w_gu[:, :FF]), cut(w_gu[:, FF:]), cut(w_down)], axis=-1)
    ff_got = swap_all(ff_pay, DP)
    seq_pay = jnp.concatenate([ff_got, w_out.reshape(8, 8, 128).transpose(1, 0, 2)], axis=-1)
    seq_got = lax.all_gather(seq_pay, SEQ, axis=1, tiled=False)
    w_gu_j = seq_got[..., : 2 * PAD].reshape(1024, 2 * PAD)
    w_down_j = seq_got[..., 2 * PAD : 3 * PAD].reshape(1024, PAD)
    w_out_j = seq_got[..., 3 * PAD :].transpose(1, 2, 0, 3).reshape(128, 1024)
    w_out_rel = jnp.concatenate(gather_dp(w_out_j))
    d_all = jnp.concatenate(gather_dp(d_out[0]))

    r1 = inv_rms(x_all)
    n1 = x_all * r1
    h = (n1 * a_gain).astype(BF)
    mixed = dot("rd,df->rf", h, w_j)
    q_raw = mixed[:, :128].reshape(8, 128, 2, 64)
    k_raw = mixed[:, 128:192].reshape(8, 128, 1, 64)
    v_raw = mixed[:, 192:].reshape(8, 128, 64)
    own_orders = lax.dynamic_slice_in_dim(orders, 2 * s, 2, 1)[b_of]
    t = np.arange(128)
    cosine, sine = angles(own_orders[:, t // 64] * 64 + t % 64)
    cosine, sine = cosine[:, :, None], sine[:, :, None]
    rq = inv_rms(q_raw)
    qn = q_raw * rq
    q_rot = rotate(qn * q_gain, cosine, sine).astype(BF)
    rk = inv_rms(k_raw)
    kn = k_raw * rk
    k_rot = rotate(kn * k_gain, cosine, sine).astype(BF)

    kv = jnp.concatenate([k_rot[:, :, 0], v_raw.astype(BF)], axis=-1)
    q_send = q_rot.reshape(8, 2, 64, 2, 64).transpose(0, 3, 2, 1, 4).reshape(8, 2, 64, 128)
    send = jnp.concatenate([jnp.broadcast_to(kv[:, None], (8, 2, 128, 128)), q_send], axis=2)
    qkv = swap_all(send[r_of].reshape(16, 192, 128), SEQ)

    keys = qkv[:, :128, :64].reshape(2048, 64)
    values = qkv[:, :128, 64:].reshape(2048, 64)
    queries = from_slots(qkv[:, 128:])
    order = lax.dynamic_index_in_dim(orders, s // 2, 0, False)
    tt = np.arange(2048)
    pos = order[tt // 64] * 64 + tt % 64
    allowed = pos[:, None] >= pos[None, :]
    scale = HD**-0.5

    def scores_of():
        return jnp.where(allowed, dot("qd,td->qt", queries, keys) * scale, -1e30)

    scores = scores_of()
    top = jnp.max(scores, axis=-1, keepdims=True)
    weights = jnp.exp(scores - top)
    total = jnp.sum(weights, axis=-1, keepdims=True)
    probs = weights / total
    o = dot("qt,td->qd", probs.astype(BF), values)
    lse = top + jnp.log(total)
    o_bf = o.astype(BF)
    o_got = swap_all(to_slots(o_bf), SEQ)
    attn_j = o_got.reshape(8, 2, 64, 2, 64).transpose(0, 3, 2, 1, 4).reshape(1024, 128)
    attn = jnp.concatenate(gather_dp(attn_j), axis=1)
    attn = attn.reshape(8, 128, 1024)[b_of].reshape(1024, 1024)

    x1 = x_all + dot("rd,de->re", attn, w_out_rel)
    r2 = inv_rms(x1)
    n2 = x1 * r2
    h2 = (n2 * f_gain).astype(BF)
    gate_up = dot("rd,dc->rc", h2, w_gu_j)
    gate = gate_up[:, :PAD]
    upper = gate_up[:, PAD:]
    sigma = jax.nn.sigmoid(gate)
    swish = gate * sigma
    act = (swish * upper).astype(BF)
    d_act = dot("rd,dc->rc", d_all, w_down_j).astype(BF).astype(F32)
    d_gate = d_act * upper * (sigma * (1.0 + gate * (1.0 - sigma)))
    d_gu = jnp.concatenate([d_gate, d_act * swish], axis=1).astype(BF)
    d_h2_part = dot("rc,dc->rd", d_gu, w_gu_j)
    d_h2_four = d_h2_part.astype(BF).reshape(4, 2, 128, 1024)
    d_h2 = scatter_dp(d_h2_four[:, 0], d_h2_four[:, 1])
    gf_part = jnp.sum(d_h2_part * n2, axis=0)
    out_part = dot("rc,dc->rd", act, w_down_j).astype(BF).reshape(4, 2, 128, 1024)
    result = x1[:128] + scatter_dp(out_part[:, 0], out_part[:, 1])
    g_gu_j = dot("rd,rc->dc", h2, d_gu)
    g_down_j = dot("rd,rc->dc", d_all, act)
    g_ff = jnp.concatenate([g_gu_j, g_down_j], axis=1).astype(BF)
    g_ff = g_ff.reshape(8, 16, 8, 3 * PAD).transpose(1, 0, 2, 3)
    g_ff = jnp.sum(swap_all(g_ff.reshape(16, 64, 3 * PAD), SEQ).astype(F32), axis=0).astype(BF)
    g_ff = swap_all(g_ff.reshape(8, 8, 3 * PAD), DP).astype(F32)
    g_ff = g_ff.reshape(8, 8, 3, PAD)[..., :UNITS].transpose(2, 1, 0, 3).reshape(3, 8, FF)
    g_gu = jnp.concatenate([g_ff[0], g_ff[1]], axis=1)
    g_down = g_ff[2]

    d_x1 = d_out[0].astype(F32) + rms_back(d_h2, n2[:128], r2[:128], f_gain)
    d_branch = d_x1.astype(BF)
    d_attn = dot("re,de->rd", d_branch, w_out_rel).astype(BF).reshape(2, 64, 8, 2, 64)
    d_attn = d_attn.transpose(2, 3, 1, 0, 4)[r_of].reshape(8, 2, 64, 128)
    d_attn = swap_all(d_attn, DP)
    d_o = from_slots(swap_all(d_attn.reshape(16, 64, 128), SEQ))
    branch_all = jnp.concatenate(gather_dp(d_branch)).reshape(8, 128, 1024)[r_of].reshape(1024, 1024)
    g_out_j = dot("rd,re->de", attn_j, branch_all)
    g_out_send = g_out_j.astype(BF).reshape(16, 8, 8, 128).transpose(0, 2, 1, 3).reshape(16, 64, 128)

    probs = jnp.exp(scores_of() - lse)
    d_probs = dot("qd,td->qt", d_o, values)
    delta = jnp.sum(d_o.astype(F32) * o, axis=-1, keepdims=True)
    d_scores = (probs * (d_probs - delta)).astype(BF)
    d_q = dot("qt,td->qd", d_scores, keys) * scale
    d_k = dot("qt,qd->td", d_scores, queries) * scale
    d_v = dot("qt,qd->td", probs.astype(BF), d_o)
    d_kv = jnp.concatenate([d_k, d_v], axis=1).astype(BF).reshape(16, 128, 128)
    back = swap_all(jnp.concatenate([d_kv, to_slots(d_q.astype(BF)), g_out_send], axis=1), SEQ)
    g_out = jnp.sum(back[:, 192:].astype(F32), axis=0)
    g_out = g_out.reshape(8, 8, 128).transpose(1, 0, 2).reshape(8, 1024)

    back = back[:, :192].reshape(8, 2, 192, 128)[b_of].astype(F32)
    d_kv = jnp.sum(back[:, :, :128], axis=1)
    d_q = back[:, :, 128:].reshape(8, 2, 64, 2, 64).transpose(0, 3, 2, 1, 4).reshape(8, 128, 2, 64)
    dq_g = unrotate(d_q, cosine, sine)
    gq_part = jnp.sum(dq_g * qn, axis=(0, 1, 2))
    dq_raw = rms_back(dq_g, qn, rq, q_gain)
    dk_g = unrotate(d_kv[:, :, None, :64], cosine, sine)
    gk_part = jnp.sum(dk_g * kn, axis=(0, 1, 2))
    dk_raw = rms_back(dk_g, kn, rk, k_gain)
    d_mixed = jnp.concatenate(
        [dq_raw.reshape(1024, 128), dk_raw.reshape(1024, 64), d_kv[:, :, 64:].reshape(1024, 64)], axis=1
    ).astype(BF)
    d_h_part = dot("rf,df->rd", d_mixed, w_j)
    ga_part = jnp.sum(d_h_part * n1, axis=0)
    d_h_four = d_h_part.astype(BF).reshape(4, 2, 128, 1024)
    d_h = scatter_dp(d_h_four[:, 0], d_h_four[:, 1])
    d_tokens = d_x1 + rms_back(d_h, n1[:128], r1[:128], a_gain)

    g_qkv_j = dot("rd,rf->df", h, d_mixed).astype(BF).reshape(128, 8, 256)
    g_gain = jnp.concatenate([ga_part, gf_part, gq_part, gk_part]).reshape(128, 17)
    gain_hi = g_gain.astype(BF)
    gain_lo = (g_gain - gain_hi.astype(F32)).astype(BF)
    gain_rows = jnp.concatenate([gain_hi, gain_lo, jnp.zeros((128, 94), BF)], axis=1)
    gain_rows = jnp.broadcast_to(gain_rows[:, None], (128, 8, 128))
    last = swap_all(
        jnp.concatenate([g_qkv_j[:, :, :128], g_qkv_j[:, :, 128:], gain_rows], axis=1), ALL
    ).astype(F32)
    g_gains = jnp.sum(last[:, 16, :17] + last[:, 16, 17:34], axis=0)
    last = jnp.sum(last.reshape(8, 16, 24, 128), axis=1)
    g_qkv = jnp.concatenate(
        [
            last[:, :8].transpose(1, 0, 2).reshape(8, 1024),
            last[:, 8:16, :64].transpose(1, 0, 2).reshape(8, 512),
            last[:, 8:16, 64:].transpose(1, 0, 2).reshape(8, 512),
        ],
        axis=1,
    )
    return (
        result.astype(BF)[None],
        d_tokens[None],
        g_qkv,
        g_out,
        g_gu,
        g_down,
        g_gains,
    )


def solution(mesh):
    split = Mesh(mesh.devices.reshape(4, 2, 4, 4), ALL)
    return jax.shard_map(
        on_device,
        mesh=split,
        in_specs=(
            P(DP, SEQ, None),
            P(ALL, None),
            P(ALL, None),
            P(ALL, None),
            P(ALL, None),
            P(ALL),
            P(DP, None),
            P(DP, SEQ, None),
        ),
        out_specs=(
            P(DP, SEQ, None),
            P(DP, SEQ, None),
            P(ALL, None),
            P(ALL, None),
            P(ALL, None),
            P(ALL, None),
            P(ALL),
        ),
        check_vma=False,
    )
```

time: 790 us -> 535 us (0.68)
  waiting for transfers between devices: 381 us -> 87.3 us
  starting transfers between devices: 10.3 us -> 111 us
  blocking collectives: 68.9 us -> 0 us
  local copies, waits for them, and re-layouts: 126 us -> 155 us
  matrix products: 99.3 us -> 71.5 us
    unnamed x11 -> x1, waiting for transfers between devices: 151 us -> 0.02 us
    reduce_scatter x5 -> x0, waiting for transfers between devices: 149 us -> none  [the longest x2 57 us: scatter_axes(): shard = lax.psum_scatter(shard, axis, scatter_dimension=dim, tiled=True)]
    all_gather x4 -> x1, waiting for transfers between devices: 70.5 us -> 0.02 us  [on_device(): seq_got = lax.all_gather(seq_pay, SEQ, axis=1, tiled=False)]
    unnamed x1 -> x0, blocking collectives: 68.9 us -> none
    ppermute x0 -> x66, starting transfers between devices: none -> 53.4 us  [the longest x5 16.3 us: gather_dp(): b = lax.ppermute(x, 'z', DOWN)]
    all_to_all x2 -> x10, starting transfers between devices: 9.22 us -> 57.2 us  [swap_all(): return lax.all_to_all(x, axes, split_axis=0, concat_axis=0, tiled=True)]
    all_to_all x2 -> x10, waiting for transfers between devices: 10.8 us -> 54.8 us  [swap_all(): return lax.all_to_all(x, axes, split_axis=0, concat_axis=0, tiled=True)]
    ppermute x0 -> x66, waiting for transfers between devices: none -> 32.5 us  [the longest x5 6.21 us: gather_dp(): b = lax.ppermute(x, 'z', DOWN)]
  transfers between devices with their start and end apart: 12 -> 77, of which waited for: 7 -> 24; matrix products, arithmetic and copies ran while one was open for 28% -> 53% of each run, Pallas kernels for 0% -> 0%
where the time goes in v1:
time: 535 us; the launch traced here: 525 us
  local copies, waits for them, and re-layouts  155 us (29%)
  starting transfers between devices  111 us (21%)
  waiting for transfers between devices  87.3 us (16%)
  other arithmetic  84.2 us (16%)
  matrix products  71.5 us (13%)
  between operations  16.9 us (3%)
    dot_general x18, matrix products, dot(): return jnp.einsum(spec, a, b, preferred_element_type=F32)  71.5 us
    all_to_all x10, starting transfers between devices, swap_all(): return lax.all_to_all(x, axes, split_axis=0, concat_axis=0, tiled=True)  57.2 us
    all_to_all x10, waiting for transfers between devices, swap_all(): return lax.all_to_all(x, axes, split_axis=0, concat_axis=0, tiled=True)  54.8 us
    unnamed x265, local copies, waits for them, and re-layouts  50.3 us
    add x1, other arithmetic, on_device(): pos = order[tt // 64] * 64 + tt % 64  19.7 us
    mul x1, local copies, waits for them, and re-layouts, scores_of(): return jnp.where(allowed, dot('qd,td->qt', queries, keys) * scale, -1e+30)  17.6 us
    ppermute x5, starting transfers between devices, gather_dp(): b = lax.ppermute(x, 'z', DOWN)  16.3 us
  transfers between devices with their start and end apart: 77, of which 24 were waited for; matrix products, arithmetic and copies ran while one was open for 53% of the time, Pallas kernels for 0%

profile of v1, /device:TPU:0, one launch (start us, length us, event | category | flops | bytes accessed | tf_op | source)
XLA Modules:
  0.0 525.4 jit_solution(145176964937717596)
XLA Ops:
  7.3 4.2 collective-permute-start.4
  15.0 5.8 %all-to-all-start.3 = ((bf16[8,8,1920]{2,1,0:T(8,128)(2,1)}), bf16[8,8,1920]{2,1,0:T(8,128)(2,1)S(1)}, u32[]{:S(2)}, u32[]{:S(2)}) async-start(bf16[8,8,1920]{2,1,0:T(8,128)(2,1)} %pad_maximum_fusion.17), calls=%async_computation.3 | async-start | bytes 491520 | tf_op jit(solution)/shard_map/all_to_all | solution.py:58
  23.9 5.0 all-to-all-done.3
  29.9 7.6 %all-to-all-start = ((bf16[128,24,128]{2,1,0:T(8,128)(2,1)}), bf16[128,24,128]{2,1,0:T(8,128)(2,1)S(1)}, u32[]{:S(2)}, u32[]{:S(2)}) async-start(bf16[128,24,128]{2,1,0:T(8,128)(2,1)} %bitcast.5), calls=%async_computation | async-start | bytes 1572864 | tf_op jit(solution)/shard_map/all_to_all | solution.py:58
  50.0 4.7 collective-permute-done.38
  87.2 6.4 %all-to-all-start.1 = ((bf16[16,192,128]{2,1,0:T(8,128)(2,1)}), bf16[16,192,128]{2,1,0:T(8,128)(2,1)S(1)}, u32[]{:S(2)}, u32[]{:S(2)}) async-start(bf16[16,192,128]{2,1,0:T(8,128)(2,1)} %bitcast.427), calls=%async_computation.1 | async-start | bytes 1572864 | tf_op jit(solution)/shard_map/all_to_all | solution.py:58
  98.4 19.7 %fusion.65 = s32[2048]{0:T(1024)S(1)} fusion(s32[2048]{0:T(1024)S(1)} %copy-done.55, pred[2048]{0:T(1024)(128)(4,1)S(1)} %copy-done.91, pred[2048]{0:T(1024)(128)(4,1)S(1)} %copy-done.90, pred[2048]{0:T(1024)(128)(4,1)S(1)} %copy-done.89, pred[2048]{0:T(1024)(128)(4,1)S(1)} %copy-done.88, pred[2048]{0:T(1024)(128)(4,1)S(1)} %copy-done.87, ...), kind=kLoop, calls=%fused_computation.276 | loop fusion | flops 67584 | bytes 80000 | tf_op jit(solution)/shard_map/add | solution.py:172
  125.6 8.1 %convolution_multiply_fusion = f32[2048,2048]{0,1:T(8,128)} fusion(bf16[2048,64]{1,0:T(8,128)(2,1)S(1)} %bitcast.418, bf16[2048,64]{0,1:T(8,128)(2,1)S(1)} %copy-done.7), kind=kOutput, calls=%fused_computation.17 | convolution fusion | flops 541065216 | bytes 17301504 | tf_op jit(solution)/shard_map/qd,td->qt/dot_general | solution.py:89
  133.7 17.6 %copy.267 = f32[2048,2048]{1,0:T(8,128)} copy(f32[2048,2048]{0,1:T(8,128)} %convolution_multiply_fusion) | data formatting | bytes 33554432 | tf_op jit(solution)/shard_map/mul | solution.py:177
  151.3 8.4 %fusion.4 = f32[2048]{0:T(1024)S(1)} fusion(f32[2048,2048]{1,0:T(8,128)} %copy.267, s32[2048]{0:T(1024)S(1)} %fusion.65), kind=kLoop, calls=%fused_computation.16 | loop fusion | flops 12580864 | bytes 16793600 | tf_op jit(solution)/shard_map/reduce_max | solution.py:180
  162.0 4.5 fusion.3
  166.5 5.8 %fusion.85 = (bf16[2048,64]{0,1:T(8,128)(2,1)S(1)}, f32[2048,64]{0,1:T(8,128)}) fusion(bf16[2048,64]{1,0:T(8,128)(2,1)S(1)} %bitcast.461, f32[2048,2048]{1,0:T(8,128)S(1)} %copy-done, f32[2048]{0:T(1024)S(1)} %fusion.3, f32[2048]{0:T(1024)S(1)} %fusion.4, s32[2048]{0:T(1024)S(1)} %fusion.65), kind=kOutput, calls=%fused_computation.317 | convolution fusion | flops 557973504 | bytes 17850368 | tf_op jit(solution)/shard_map/qt,td->qd/dot_general | solution.py:89
  176.6 7.3 %all-to-all-start.2 = ((bf16[16,64,128]{2,1,0:T(8,128)(2,1)}), bf16[16,64,128]{2,1,0:T(8,128)(2,1)S(1)}, u32[]{:S(2)}, u32[]{:S(2)}) async-start(bf16[16,64,128]{2,1,0:T(8,128)(2,1)} %reshape.514), calls=%async_computation.2 | async-start | bytes 524288 | tf_op jit(solution)/shard_map/all_to_all | solution.py:58
  248.5 4.0 fusion.8
  252.5 6.6 %multiply_reduce_fusion = (f32[1024]{0:T(1024)}, bf16[1024,1024]{1,0:T(8,128)(2,1)}) fusion(f32[1024,1024]{1,0:T(8,128)S(1)} %broadcast_multiply_fusion, bf16[1024,1280]{1,0:T(8,128)(2,1)S(1)} %bitcast.430, bf16[1024,640]{1,0:T(8,128)(2,1)} %get-tuple-element.15, bf16[1024,640]{1,0:T(8,128)(2,1)S(1)} %get-tuple-element.14), kind=kOutput, calls=%fused_computation.23 | convolution fusion | flops 2692742144 | bytes 11538432 | tf_op jit(solution)/shard_map/rc,dc->rd/dot_general | solution.py:89
  260.7 5.6 %fusion.2 = bf16[2048,2048]{1,0:T(8,128)(2,1)} fusion(f32[2048,2048]{0,1:T(8,128)S(1)} %bitcast.409, f32[2048]{0:T(1024)S(1)} %log_add_fusion, s32[2048]{0:T(1024)S(1)} %fusion.65), kind=kLoop, calls=%fused_computation.10 | loop fusion | flops 16777216 | bytes 25182208 | tf_op jit(solution)/shard_map/convert_element_type | solution.py:237
  268.0 4.4 convolution_convert_fusion
  300.8 4.6 all-to-all-start.4
  308.4 4.7 all-to-all-done.4
  313.1 5.0 all-to-all-start.5
  336.6 9.3 %multiply_convert_fusion = bf16[2048,2048]{1,0:T(8,128)(2,1)S(1)} fusion(f32[2048,2048]{1,0:T(8,128)} %copy.267, bf16[2048,64]{0,1:T(8,128)(2,1)S(1)} %reshape.531, bf16[2048,64]{1,0:T(8,128)(2,1)} %bitcast.460, f32[2048]{0:T(1024)S(1)} %multiply_reduce_fusion.5, f32[2048]{0:T(1024)S(1)} %log_add_fusion, s32[2048]{0:T(1024)S(1)} %fusion.65), kind=kOutput, calls=%fused_computation.11 | convolution fusion | flops 562036736 | bytes 25714688 | tf_op jit(solution)/shard_map/qd,td->qt/dot_general | solution.py:89
  351.4 6.1 %convolution_convert_fusion.6 = bf16[16,128,64]{1,2,0:T(8,128)(2,1)S(1)} fusion(bf16[16,128,2048]{2,1,0:T(8,128)(2,1)} %bitcast.410, bf16[2048,64,1]{0,1,2:T(8,128)(2,1)S(1)} %reshape.738), kind=kOutput, calls=%fused_computation.59 | convolution fusion | flops 537001984 | bytes 8912896 | tf_op jit(solution)/shard_map/qt,qd->td/dot_general | solution.py:89
  370.2 3.8 gather_fusion.5
  380.3 7.2 %all-to-all-start.6 = ((bf16[16,256,128]{1,2,0:T(8,128)(2,1)}), bf16[16,256,128]{1,2,0:T(8,128)(2,1)S(1)}, u32[]{:S(2)}, u32[]{:S(2)}) async-start(bf16[16,256,128]{1,2,0:T(8,128)(2,1)} %pad_maximum_fusion.4), calls=%async_computation.6 | async-start | bytes 2097152 | tf_op jit(solution)/shard_map/all_to_all | solution.py:58
  387.6 3.9 convolution_convert_fusion.2
  407.0 4.9 all-to-all-start.8
  428.8 3.9 multiply_reduce_fusion.1
  436.2 26.8 %all-to-all-done.8 = bf16[16,64,1920]{2,1,0:T(8,128)(2,1)} async-done(((bf16[16,64,1920]{2,1,0:T(8,128)(2,1)}), bf16[16,64,1920]{2,1,0:T(8,128)(2,1)}, u32[]{:S(2)}, u32[]{:S(2)}) %all-to-all-start.8) | async-done | bytes 3932192 | tf_op jit(solution)/shard_map/all_to_all | solution.py:58
  463.0 4.6 all-to-all-start.7
  476.0 7.9 %all-to-all-done.7 = bf16[128,24,128]{2,1,0:T(8,128)(2,1)S(1)} async-done(((bf16[128,24,128]{2,1,0:T(8,128)(2,1)}), bf16[128,24,128]{2,1,0:T(8,128)(2,1)S(1)}, u32[]{:S(2)}, u32[]{:S(2)}) %all-to-all-start.7) | async-done | bytes 786464 | tf_op jit(solution)/shard_map/all_to_all | solution.py:58
  489.5 5.4 %all-to-all-done.9 = bf16[8,8,1920]{2,1,0:T(8,128)(2,1)S(1)} async-done(((bf16[8,8,1920]{2,1,0:T(8,128)(2,1)}), bf16[8,8,1920]{2,1,0:T(8,128)(2,1)S(1)}, u32[]{:S(2)}, u32[]{:S(2)}) %all-to-all-start.9) | async-done | bytes 245792 | tf_op jit(solution)/shard_map/all_to_all | solution.py:58
  506.0 3.9 collective-permute-done.61
  (618 shorter events, 280.6 us)
Async XLA Ops:
  7.3 31.1 %collective-permute-start.4 = (bf16[128,1024]{1,0:T(8,128)(2,1)}, bf16[128,1024]{1,0:T(8,128)(2,1)}, u32[]{:S(2)}, u32[]{:S(2)}) collective-permute-start(bf16[128,1024]{1,0:T(8,128)(2,1)} %bitcast.463), channel_id=1, source_target_pairs={{0,96},{32,0},{64,32},{96,64},{1,97},{33,1},{65,33},{97,65},{2,98}... | collective-permute-start | bytes 786440 | tf_op jit(solution)/shard_map/ppermute | solution.py:35
  11.4 30.7 %collective-permute-start.1 = (bf16[128,1024]{1,0:T(8,128)(2,1)}, bf16[128,1024]{1,0:T(8,128)(2,1)}, u32[]{:S(2)}, u32[]{:S(2)}) collective-permute-start(bf16[128,1024]{1,0:T(8,128)(2,1)} %bitcast.464), channel_id=1, source_target_pairs={{0,32},{32,64},{64,96},{96,0},{1,33},{33,65},{65,97},{97,1},{2,34}... | collective-permute-start | bytes 786440 | tf_op jit(solution)/shard_map/ppermute | solution.py:34
  11.4 31.4 %collective-permute-start = (bf16[128,1024]{1,0:T(8,128)(2,1)}, bf16[128,1024]{1,0:T(8,128)(2,1)}, u32[]{:S(2)}, u32[]{:S(2)}) collective-permute-start(bf16[128,1024]{1,0:T(8,128)(2,1)} %bitcast.465), channel_id=1, source_target_pairs={{0,16},{16,0},{1,17},{17,1},{2,18},{18,2},{3,19},{19,3},{4,20},{20... | collective-permute-start | bytes 786440 | tf_op jit(solution)/shard_map/ppermute | solution.py:38
  11.5 34.2 %collective-permute-start.35 = (bf16[128,1024]{1,0:T(8,128)(2,1)}, bf16[128,1024]{1,0:T(8,128)(2,1)}, u32[]{:S(2)}, u32[]{:S(2)}) collective-permute-start(bf16[128,1024]{1,0:T(8,128)(2,1)} %bitcast.450), channel_id=1, source_target_pairs={{0,32},{32,64},{64,96},{96,0},{1,33},{33,65},{65,97},{97,1},{2,34}... | collective-permute-start | bytes 786440 | tf_op jit(solution)/shard_map/ppermute | solution.py:34
  11.5 35.7 %collective-permute-start.34 = (bf16[128,1024]{1,0:T(8,128)(2,1)}, bf16[128,1024]{1,0:T(8,128)(2,1)}, u32[]{:S(2)}, u32[]{:S(2)}) collective-permute-start(bf16[128,1024]{1,0:T(8,128)(2,1)} %bitcast.451), channel_id=1, source_target_pairs={{0,16},{16,0},{1,17},{17,1},{2,18},{18,2},{3,19},{19,3},{4,20},{20... | collective-permute-start | bytes 786440 | tf_op jit(solution)/shard_map/ppermute | solution.py:38
  29.9 36.6 %all-to-all-start = ((bf16[128,24,128]{2,1,0:T(8,128)(2,1)}), bf16[128,24,128]{2,1,0:T(8,128)(2,1)S(1)}, u32[]{:S(2)}, u32[]{:S(2)}) async-start(bf16[128,24,128]{2,1,0:T(8,128)(2,1)} %bitcast.5), calls=%async_computation | async-start | bytes 1572864 | tf_op jit(solution)/shard_map/all_to_all | solution.py:58
  37.5 177.6 %all-gather.3.cloned.1.call-start = ((), (), s32[]{:S(2)}) async-start(), calls=%async_computation.10 | async-start | bytes 4456448 | tf_op jit(solution)/shard_map/all_gather | solution.py:137
  38.3 16.4 %collective-permute-start.38 = (bf16[128,1024]{1,0:T(8,128)(2,1)S(1)}, bf16[128,1024]{1,0:T(8,128)(2,1)}, u32[]{:S(2)}, u32[]{:S(2)}) collective-permute-start(bf16[128,1024]{1,0:T(8,128)(2,1)S(1)} %bitcast.452), channel_id=1, source_target_pairs={{0,96},{32,0},{64,32},{96,64},{1,97},{33,1},{65,33},{97,65},{2,98}... | collective-permute-start | bytes 786440 | tf_op jit(solution)/shard_map/ppermute | solution.py:35
  42.1 19.7 %collective-permute-start.5 = (bf16[64,1024]{1,0:T(8,128)(2,1)S(1)}, bf16[64,1024]{1,0:T(8,128)(2,1)S(1)}, u32[]{:S(2)}, u32[]{:S(2)}) collective-permute-start(bf16[64,1024]{1,0:T(8,128)(2,1)S(1)} %slice.465), channel_id=1, source_target_pairs={{0,96},{32,0},{64,32},{96,64},{1,97},{33,1},{65,33},{97,65},{2,98}... | collective-permute-start | bytes 393224 | tf_op jit(solution)/shard_map/ppermute | solution.py:37
  42.8 16.2 %collective-permute-start.2 = (bf16[128,1024]{1,0:T(8,128)(2,1)}, bf16[128,1024]{1,0:T(8,128)(2,1)S(1)}, u32[]{:S(2)}, u32[]{:S(2)}) collective-permute-start(bf16[128,1024]{1,0:T(8,128)(2,1)} %collective-permute-done.1), channel_id=1, source_target_pairs={{0,16},{16,0},{1,17},{17,1},{2,18},{18,2},{3,19},{19,3},{4,20},{20... | collective-permute-start | bytes 786440 | tf_op jit(solution)/shard_map/ppermute | solution.py:38
  45.7 15.7 %collective-permute-start.3 = (bf16[64,1024]{1,0:T(8,128)(2,1)S(1)}, bf16[64,1024]{1,0:T(8,128)(2,1)S(1)}, u32[]{:S(2)}, u32[]{:S(2)}) collective-permute-start(bf16[64,1024]{1,0:T(8,128)(2,1)S(1)} %slice.464), channel_id=1, source_target_pairs={{0,32},{32,64},{64,96},{96,0},{1,33},{33,65},{65,97},{97,1},{2,34}... | collective-permute-start | bytes 393224 | tf_op jit(solution)/shard_map/ppermute | solution.py:36
  61.4 125.8 %collective-permute-start.42 = (bf16[128,1024]{1,0:T(8,128)(2,1)}, bf16[128,1024]{1,0:T(8,128)(2,1)}, u32[]{:S(2)}, u32[]{:S(2)}) collective-permute-start(bf16[128,1024]{1,0:T(8,128)(2,1)} %collective-permute-done.38), channel_id=1, source_target_pairs={{0,16},{16,0},{1,17},{17,1},{2,18},{18,2},{3,19},{19,3},{4,20},{20... | collective-permute-start | bytes 786440 | tf_op jit(solution)/shard_map/ppermute | solution.py:38
  64.1 31.0 %collective-permute-start.40 = (bf16[64,1024]{1,0:T(8,128)(2,1)}, bf16[64,1024]{1,0:T(8,128)(2,1)}, u32[]{:S(2)}, u32[]{:S(2)}) collective-permute-start(bf16[64,1024]{1,0:T(8,128)(2,1)} %collective-permute-done.37), channel_id=1, source_target_pairs={{0,16},{16,0},{1,17},{17,1},{2,18},{18,2},{3,19},{19,3},{4,20},{20... | collective-permute-start | bytes 393224 | tf_op jit(solution)/shard_map/ppermute | solution.py:38
  64.2 119.8 %collective-permute-start.41 = (bf16[64,1024]{1,0:T(8,128)(2,1)}, bf16[64,1024]{1,0:T(8,128)(2,1)}, u32[]{:S(2)}, u32[]{:S(2)}) collective-permute-start(bf16[64,1024]{1,0:T(8,128)(2,1)} %collective-permute-done.39), channel_id=1, source_target_pairs={{0,16},{16,0},{1,17},{17,1},{2,18},{18,2},{3,19},{19,3},{4,20},{20... | collective-permute-start | bytes 393224 | tf_op jit(solution)/shard_map/ppermute | solution.py:38
  87.2 31.0 %all-to-all-start.1 = ((bf16[16,192,128]{2,1,0:T(8,128)(2,1)}), bf16[16,192,128]{2,1,0:T(8,128)(2,1)S(1)}, u32[]{:S(2)}, u32[]{:S(2)}) async-start(bf16[16,192,128]{2,1,0:T(8,128)(2,1)} %bitcast.427), calls=%async_computation.1 | async-start | bytes 1572864 | tf_op jit(solution)/shard_map/all_to_all | solution.py:58
  176.6 15.8 %all-to-all-start.2 = ((bf16[16,64,128]{2,1,0:T(8,128)(2,1)}), bf16[16,64,128]{2,1,0:T(8,128)(2,1)S(1)}, u32[]{:S(2)}, u32[]{:S(2)}) async-start(bf16[16,64,128]{2,1,0:T(8,128)(2,1)} %reshape.514), calls=%async_computation.2 | async-start | bytes 524288 | tf_op jit(solution)/shard_map/all_to_all | solution.py:58
  285.3 20.1 %collective-permute-start.27 = (bf16[4,128,1024]{2,1,0:T(8,128)(2,1)}, bf16[4,128,1024]{2,1,0:T(8,128)(2,1)}, u32[]{:S(2)}, u32[]{:S(2)}) collective-permute-start(bf16[4,128,1024]{2,1,0:T(8,128)(2,1)} %slice_bitcast_fusion.4), channel_id=1, source_target_pairs={{0,16},{16,0},{1,17},{17,1},{2,18},{18,2},{3,19},{19,3},{4,20},{20... | collective-permute-start | bytes 3145736 | tf_op jit(solution)/shard_map/ppermute | solution.py:44
  288.1 32.4 %collective-permute-start.54 = (bf16[128,1024]{1,0:T(8,128)(2,1)S(1)}, bf16[128,1024]{1,0:T(8,128)(2,1)}, u32[]{:S(2)}, u32[]{:S(2)}) collective-permute-start(bf16[128,1024]{1,0:T(8,128)(2,1)S(1)} %get-tuple-element.12), channel_id=1, source_target_pairs={{0,96},{32,0},{64,32},{96,64},{1,97},{33,1},{65,33},{97,65},{2,98}... | collective-permute-start | bytes 786440 | tf_op jit(solution)/shard_map/ppermute | solution.py:35
  291.8 32.4 %collective-permute-start.51 = (bf16[128,1024]{1,0:T(8,128)(2,1)S(1)}, bf16[128,1024]{1,0:T(8,128)(2,1)}, u32[]{:S(2)}, u32[]{:S(2)}) collective-permute-start(bf16[128,1024]{1,0:T(8,128)(2,1)S(1)} %get-tuple-element.12), channel_id=1, source_target_pairs={{0,32},{32,64},{64,96},{96,0},{1,33},{33,65},{65,97},{97,1},{2,34}... | collective-permute-start | bytes 786440 | tf_op jit(solution)/shard_map/ppermute | solution.py:34
  291.8 33.5 %collective-permute-start.50 = (bf16[128,1024]{1,0:T(8,128)(2,1)S(1)}, bf16[128,1024]{1,0:T(8,128)(2,1)}, u32[]{:S(2)}, u32[]{:S(2)}) collective-permute-start(bf16[128,1024]{1,0:T(8,128)(2,1)S(1)} %get-tuple-element.12), channel_id=1, source_target_pairs={{0,16},{16,0},{1,17},{17,1},{2,18},{18,2},{3,19},{19,3},{4,20},{20... | collective-permute-start | bytes 786440 | tf_op jit(solution)/shard_map/ppermute | solution.py:38
  313.1 18.6 %all-to-all-start.5 = ((bf16[16,64,128]{2,1,0:T(8,128)(2,1)}), bf16[16,64,128]{2,1,0:T(8,128)(2,1)S(1)}, u32[]{:S(2)}, u32[]{:S(2)}) async-start(bf16[16,64,128]{2,1,0:T(8,128)(2,1)} %bitcast.95), calls=%async_computation.5 | async-start | bytes 524288 | tf_op jit(solution)/shard_map/all_to_all | solution.py:58
  320.0 73.2 %collective-permute-start.28 = (bf16[64,1024]{1,0:T(8,128)(2,1)}, bf16[64,1024]{1,0:T(8,128)(2,1)S(1)}, u32[]{:S(2)}, u32[]{:S(2)}) collective-permute-start(bf16[64,1024]{1,0:T(8,128)(2,1)} %get-tuple-element.38), channel_id=1, source_target_pairs={{0,32},{32,64},{64,96},{96,0},{1,33},{33,65},{65,97},{97,1},{2,34}... | collective-permute-start | bytes 393224 | tf_op jit(solution)/shard_map/ppermute | solution.py:46
  325.2 43.4 %collective-permute-start.58 = (bf16[128,1024]{1,0:T(8,128)(2,1)}, bf16[128,1024]{1,0:T(8,128)(2,1)}, u32[]{:S(2)}, u32[]{:S(2)}) collective-permute-start(bf16[128,1024]{1,0:T(8,128)(2,1)} %collective-permute-done.54), channel_id=1, source_target_pairs={{0,16},{16,0},{1,17},{17,1},{2,18},{18,2},{3,19},{19,3},{4,20},{20... | collective-permute-start | bytes 786440 | tf_op jit(solution)/shard_map/ppermute | solution.py:38
  325.3 33.7 %collective-permute-start.52 = (bf16[128,1024]{1,0:T(8,128)(2,1)}, bf16[128,1024]{1,0:T(8,128)(2,1)}, u32[]{:S(2)}, u32[]{:S(2)}) collective-permute-start(bf16[128,1024]{1,0:T(8,128)(2,1)} %collective-permute-done.51), channel_id=1, source_target_pairs={{0,16},{16,0},{1,17},{17,1},{2,18},{18,2},{3,19},{19,3},{4,20},{20... | collective-permute-start | bytes 786440 | tf_op jit(solution)/shard_map/ppermute | solution.py:38
  329.2 36.2 %collective-permute-start.57 = (bf16[64,1024]{1,0:T(8,128)(2,1)}, bf16[64,1024]{1,0:T(8,128)(2,1)}, u32[]{:S(2)}, u32[]{:S(2)}) collective-permute-start(bf16[64,1024]{1,0:T(8,128)(2,1)} %collective-permute-done.55), channel_id=1, source_target_pairs={{0,16},{16,0},{1,17},{17,1},{2,18},{18,2},{3,19},{19,3},{4,20},{20... | collective-permute-start | bytes 393224 | tf_op jit(solution)/shard_map/ppermute | solution.py:38
  331.5 32.3 %collective-permute-start.56 = (bf16[64,1024]{1,0:T(8,128)(2,1)}, bf16[64,1024]{1,0:T(8,128)(2,1)}, u32[]{:S(2)}, u32[]{:S(2)}) collective-permute-start(bf16[64,1024]{1,0:T(8,128)(2,1)} %collective-permute-done.53), channel_id=1, source_target_pairs={{0,16},{16,0},{1,17},{17,1},{2,18},{18,2},{3,19},{19,3},{4,20},{20... | collective-permute-start | bytes 393224 | tf_op jit(solution)/shard_map/ppermute | solution.py:38
  380.3 25.7 %all-to-all-start.6 = ((bf16[16,256,128]{1,2,0:T(8,128)(2,1)}), bf16[16,256,128]{1,2,0:T(8,128)(2,1)S(1)}, u32[]{:S(2)}, u32[]{:S(2)}) async-start(bf16[16,256,128]{1,2,0:T(8,128)(2,1)} %pad_maximum_fusion.4), calls=%async_computation.6 | async-start | bytes 2097152 | tf_op jit(solution)/shard_map/all_to_all | solution.py:58
  398.4 69.3 %collective-permute-start.31 = (bf16[64,1024]{1,0:T(8,128)(2,1)}, bf16[64,1024]{1,0:T(8,128)(2,1)}, u32[]{:S(2)}, u32[]{:S(2)}) collective-permute-start(bf16[64,1024]{1,0:T(8,128)(2,1)} %get-tuple-element.40), channel_id=1, source_target_pairs={{0,32},{32,64},{64,96},{96,0},{1,33},{33,65},{65,97},{97,1},{2,34}... | collective-permute-start | bytes 393224 | tf_op jit(solution)/shard_map/ppermute | solution.py:48
  402.2 65.5 %collective-permute-start.33 = (bf16[64,1024]{1,0:T(8,128)(2,1)}, bf16[64,1024]{1,0:T(8,128)(2,1)}, u32[]{:S(2)}, u32[]{:S(2)}) collective-permute-start(bf16[64,1024]{1,0:T(8,128)(2,1)} %get-tuple-element.37), channel_id=1, source_target_pairs={{0,96},{32,0},{64,32},{96,64},{1,97},{33,1},{65,33},{97,65},{2,98}... | collective-permute-start | bytes 393224 | tf_op jit(solution)/shard_map/ppermute | solution.py:51
  407.0 56.0 %all-to-all-start.8 = ((bf16[16,64,1920]{2,1,0:T(8,128)(2,1)}), bf16[16,64,1920]{2,1,0:T(8,128)(2,1)}, u32[]{:S(2)}, u32[]{:S(2)}) async-start(bf16[16,64,1920]{2,1,0:T(8,128)(2,1)} %copy_bitcast_fusion), calls=%async_computation.8 | async-start | bytes 7864320 | tf_op jit(solution)/shard_map/all_to_all | solution.py:58
  463.0 21.0 %all-to-all-start.7 = ((bf16[128,24,128]{2,1,0:T(8,128)(2,1)}), bf16[128,24,128]{2,1,0:T(8,128)(2,1)S(1)}, u32[]{:S(2)}, u32[]{:S(2)}) async-start(bf16[128,24,128]{2,1,0:T(8,128)(2,1)} %pad_maximum_fusion.6), calls=%async_computation.7 | async-start | bytes 1572864 | tf_op jit(solution)/shard_map/all_to_all | solution.py:58
  471.7 23.3 %collective-permute-start.59 = (bf16[4,128,1024]{2,1,0:T(8,128)(2,1)}, bf16[4,128,1024]{2,1,0:T(8,128)(2,1)}, u32[]{:S(2)}, u32[]{:S(2)}) collective-permute-start(bf16[4,128,1024]{2,1,0:T(8,128)(2,1)} %slice_bitcast_fusion), channel_id=1, source_target_pairs={{0,16},{16,0},{1,17},{17,1},{2,18},{18,2},{3,19},{19,3},{4,20},{20... | collective-permute-start | bytes 3145736 | tf_op jit(solution)/shard_map/ppermute | solution.py:44
  (154 other events, 1399.3 us)
Sparse Core Ops, SparseCore 0:
  41.1 52.5 all-gather.2
